TPU v7x, 512 devices: a whole 4x8x8 slice. The times are simulated.
512 devices in a mesh: rep: 8 (over x, core), exp: 64 (over z, y).
Axes of the slice: x: 4, y: 8, z: 8, core: 2. Of those that a mesh axis runs over, the one named last changes fastest.
Arguments:
- hidden: bfloat16 [8, 64, 320, 768], P('rep', 'exp'), may hold values from -6 to 6
- down_weight: bfloat16 [64, 768, 4096], P('exp', None, 'rep'), may hold values from -0.21875 to 0.21875
- grad_out: bfloat16 [65536, 4096], P(('rep', 'exp')), may hold values from -6 to 6
- expert_ids: int32 [65536, 2], P(('rep', 'exp')), may hold values from 0 to 63, all different within a row; in each aligned block of 128 rows (0 to 127, 128 to 255, ...) at most 5 rows name the same one
- gate_weights: float32 [65536, 2], P(('rep', 'exp')), may hold values from 0.03 to 0.4
Outputs:
- combined: bfloat16 [65536, 4096], P(('rep', 'exp'))
- hidden_grad: bfloat16 [8, 64, 320, 768], P('rep', 'exp')
- weight_grad: bfloat16 [64, 768, 4096], P('exp', None, 'rep')
- gate_grad: float32 [65536, 2], P(('rep', 'exp'))
Inputs may be any that keep to these rules, and one draw needn't show every extreme that they name: `expert_ids`: A token names 2 different experts. Within the 128 tokens of one device no expert is named more than 5 times, a bound that some block reaches.
All inputs are finite; a program needn't handle non-finite values.
Results may differ from a plain program's by a relative error of at most 0.014.
Values may be sent and summed in bfloat16 or wider, within the bound.
A program may use at most 64 MiB of HBM per device.

v0:
```python
import jax
import jax.numpy as jnp
from jax import lax
from jax.sharding import PartitionSpec as P


def slot_tables(routed, gate_weights, expert_count, capacity):
    token_count = routed.shape[0]
    matches = (routed[:, :, None] == jnp.arange(expert_count, dtype=jnp.int32)).astype(jnp.int32)
    per_token = jnp.sum(matches, axis=1)
    before = jnp.cumsum(per_token, axis=0) - per_token
    position = jnp.sum(matches * before[:, None, :], axis=2)
    target = routed * capacity + position
    matched = target[:, :, None] == jnp.arange(expert_count * capacity, dtype=jnp.int32)
    token_index = jnp.arange(token_count, dtype=jnp.int32)[:, None, None]
    slot_token = jnp.sum(jnp.where(matched, token_index, 0), axis=(0, 1))
    slot_gate = jnp.sum(jnp.where(matched, gate_weights[:, :, None], 0.0), axis=(0, 1))
    return (target, slot_token, slot_gate)


def per_device(hidden, down_weight, grad_out, expert_ids, gate_weights):
    rep_count = lax.axis_size("rep")
    exp_count = lax.axis_size("exp")
    slots_all = hidden.shape[2]
    capacity = slots_all // exp_count
    token_count, model_width = grad_out.shape
    top_count = expert_ids.shape[1]
    slice_width = model_width // rep_count
    target, slot_token, slot_gate = slot_tables(expert_ids, gate_weights, exp_count, capacity)
    weights_local = down_weight[0]
    grad_split = (
        grad_out.reshape(token_count, rep_count, slice_width).transpose(1, 0, 2).astype(jnp.float32)
    )
    outgoing = (jnp.take(grad_split, slot_token, axis=1) * slot_gate[None, :, None]).astype(
        jnp.bfloat16
    )
    outgoing = outgoing.reshape(rep_count, exp_count, capacity, slice_width)
    arrived = lax.all_to_all(
        lax.all_to_all(outgoing, "exp", split_axis=1, concat_axis=1, tiled=True),
        "rep",
        split_axis=0,
        concat_axis=0,
        tiled=True,
    )
    arrived = arrived.reshape(rep_count, slots_all, slice_width)
    gathered = lax.all_gather(hidden[0], "rep", axis=0, tiled=True)
    outputs = jnp.einsum(
        "rnf,fd->rnd", gathered, weights_local, preferred_element_type=jnp.float32
    ).astype(jnp.bfloat16)
    outputs = outputs.reshape(rep_count, exp_count, capacity, slice_width)
    returned = lax.all_to_all(
        lax.all_to_all(outputs, "exp", split_axis=1, concat_axis=1, tiled=True),
        "rep",
        split_axis=0,
        concat_axis=0,
        tiled=True,
    )
    returned = returned.reshape(rep_count, exp_count * capacity, slice_width)
    weight_grad = jnp.einsum(
        "rnf,rnd->fd", gathered, arrived, preferred_element_type=jnp.float32
    ).astype(jnp.bfloat16)[None]
    hidden_sum = lax.psum_scatter(
        jnp.einsum(
            "rnd,fd->rnf", arrived, weights_local, preferred_element_type=jnp.float32
        ).astype(jnp.bfloat16),
        "rep",
        scatter_dimension=0,
        tiled=True,
    )
    hidden_grad = hidden_sum[None]
    picked = jnp.take(returned, target.reshape(-1), axis=1)
    picked = picked.reshape(rep_count, token_count, top_count, slice_width).transpose(1, 2, 0, 3)
    picked = picked.reshape(token_count, top_count, model_width).astype(jnp.float32)
    combined = jnp.sum(gate_weights[:, :, None] * picked, axis=1).astype(jnp.bfloat16)
    gate_grad = jnp.sum(grad_out.astype(jnp.float32)[:, None, :] * picked, axis=2)
    return (combined, hidden_grad, weight_grad, gate_grad)


def solution(mesh):
    return jax.shard_map(
        per_device,
        mesh=mesh,
        in_specs=(
            P("rep", "exp", None, None),
            P("exp", None, "rep"),
            P(("rep", "exp"), None),
            P(("rep", "exp"), None),
            P(("rep", "exp"), None),
        ),
        out_specs=(
            P(("rep", "exp"), None),
            P("rep", "exp", None, None),
            P("exp", None, "rep"),
            P(("rep", "exp"), None),
        ),
        check_vma=False,
    )
```

profile of v0, /device:TPU:112, one launch (start us, length us, event | category | flops | bytes accessed | tf_op | source)
XLA Modules:
  0.0 299.4 jit_solution(2312357851779008377)
XLA Ops:
  7.2 0.0 copy-start
  7.2 0.8 convert_reduce_fusion
  7.9 0.1 copy.60
  8.0 0.2 reduce_window_sum.11
  8.2 0.1 copy.62
  8.3 0.7 select_reduce_fusion.2
  9.0 0.7 compare_and_fusion.1
  9.7 0.1 select_reduce_fusion.1
  9.9 0.1 reduce_sum.62
  10.0 0.8 select_reduce_fusion
  10.9 0.1 mul.51
  11.0 1.6 copy.75
  12.7 3.5 %gather_fusion.1 = f32[320,8,512]{2,1,0:T(8,128)} fusion(f32[8,128,512]{2,0,1:T(8,128)S(1)} %bitcast.43, s32[1024]{0:T(1024)S(1)} %pad_clamp_fusion), kind=kCustom, calls=%fused_computation.1 | custom fusion | bytes 10487040 | tf_op jit(solution)/shard_map/jit(_take)/gather | solution.py:34
  16.2 4.1 %multiply_convert_fusion = bf16[8,64,5,512]{3,0,2,1:T(8,128)(2,1)} fusion(f32[8,64,5,512]{3,0,2,1:T(8,128)} %bitcast.45, f32[64,5]{1,0:T(8,128)S(1)} %mul.51, pred[64,5]{1,0:T(8,128)(4,1)S(1)} %compare_and_fusion), kind=kLoop, calls=%fused_computation.2 | loop fusion | flops 3932160 | bytes 7865920 | tf_op jit(solution)/shard_map/convert_element_type | solution.py:34
  20.3 15.3 %all-to-all-start.2 = ((bf16[8,64,5,512]{3,0,2,1:T(8,128)(2,1)}), bf16[8,64,5,512]{3,0,2,1:T(8,128)(2,1)}, u32[]{:S(2)}, u32[]{:S(2)}) async-start(bf16[8,64,5,512]{3,0,2,1:T(8,128)(2,1)} %multiply_convert_fusion), calls=%async_computation.2 | async-start | bytes 5242880 | tf_op jit(solution)/shard_map/all_to_all | solution.py:39
  35.5 0.0 all-gather.3.cloned.1.call-start
  35.6 0.7 all-gather.3.cloned.1.call-update
  36.3 73.5 %all-to-all-done.2 = bf16[8,64,5,512]{3,0,2,1:T(8,128)(2,1)} async-done(((bf16[8,64,5,512]{3,0,2,1:T(8,128)(2,1)}), bf16[8,64,5,512]{3,0,2,1:T(8,128)(2,1)}, u32[]{:S(2)}, u32[]{:S(2)}) %all-to-all-start.2) | async-done | bytes 2621472 | tf_op jit(solution)/shard_map/all_to_all | solution.py:39
  109.8 4.2 %copy.68 = bf16[8,64,5,512]{3,1,2,0:T(8,128)(2,1)} copy(bf16[8,64,5,512]{3,0,2,1:T(8,128)(2,1)} %all-to-all-done.2) | data formatting | bytes 5242880 | tf_op jit(solution)/shard_map/all_to_all | solution.py:39
  114.0 4.4 %all-to-all-start.3 = ((bf16[8,64,5,512]{3,1,2,0:T(8,128)(2,1)}), bf16[8,64,5,512]{3,1,2,0:T(8,128)(2,1)}, u32[]{:S(2)}, u32[]{:S(2)}) async-start(bf16[8,64,5,512]{3,1,2,0:T(8,128)(2,1)} %copy.68), calls=%async_computation.3 | async-start | bytes 5242880 | tf_op jit(solution)/shard_map/all_to_all | solution.py:38
  118.4 0.0 all-gather.3.cloned.1.call-done
  118.4 0.0 copy-done
  118.4 4.3 %convolution_convert_fusion = bf16[8,320,512]{2,1,0:T(8,128)(2,1)S(1)} fusion(bf16[1,768,512]{2,1,0:T(8,128)(2,1)S(1)} %copy-done, bf16[8,1,320,768]{3,2,1,0:T(8,128)(2,1)} %all-gather.3.cloned.1.call-done), kind=kOutput, calls=%fused_computation.13 | convolution fusion | flops 2014576640 | bytes 7340032 | tf_op jit(solution)/shard_map/rnf,fd->rnd/dot_general | solution.py:47
  122.8 2.9 copy.64
  125.7 25.5 %all-to-all-done.3 = bf16[8,64,5,512]{3,1,2,0:T(8,128)(2,1)} async-done(((bf16[8,64,5,512]{3,1,2,0:T(8,128)(2,1)}), bf16[8,64,5,512]{3,1,2,0:T(8,128)(2,1)}, u32[]{:S(2)}, u32[]{:S(2)}) %all-to-all-start.3) | async-done | bytes 2621472 | tf_op jit(solution)/shard_map/all_to_all | solution.py:38
  151.2 7.9 %all-to-all-start = ((bf16[8,64,5,512]{3,0,2,1:T(8,128)(2,1)}), bf16[8,64,5,512]{3,0,2,1:T(8,128)(2,1)}, u32[]{:S(2)}, u32[]{:S(2)}) async-start(bf16[8,64,5,512]{3,0,2,1:T(8,128)(2,1)} %bitcast.46), calls=%async_computation | async-start | bytes 5242880 | tf_op jit(solution)/shard_map/all_to_all | solution.py:52
  159.1 0.2 reduce-scatter.2.cloned.1.call-start
  159.3 3.2 %copy.69 = bf16[8,64,5,512]{3,0,2,1:T(8,128)(2,1)S(1)} copy(bf16[8,64,5,512]{3,1,2,0:T(8,128)(2,1)} %all-to-all-done.3) | data formatting | bytes 5242880 | tf_op jit(solution)/shard_map/all_to_all | solution.py:38
  162.5 0.0 copy-start.1
  162.5 1.6 copy-done.1
  164.1 5.1 %fusion.6 = bf16[8,320,768]{2,1,0:T(8,128)(2,1)} fusion(bf16[8,320,512]{2,0,1:T(8,128)(2,1)S(1)} %bitcast.50, bf16[1,768,512]{2,1,0:T(8,128)(2,1)S(1)} %copy-done), kind=kOutput, calls=%fused_computation.11 | convolution fusion | flops 2015232000 | bytes 7340032 | tf_op jit(solution)/shard_map/rnd,fd->rnf/dot_general | solution.py:63
  169.2 0.0 copy-start.2
  169.2 0.0 reduce-scatter.2.cloned.1.call-update
  169.3 0.1 copy.67
  169.4 0.5 copy-done.2
  169.9 0.1 copy.59
  170.0 0.1 copy.63
  170.2 0.1 reshape.106
  170.3 53.1 %all-to-all-done = bf16[8,64,5,512]{3,0,2,1:T(8,128)(2,1)} async-done(((bf16[8,64,5,512]{3,0,2,1:T(8,128)(2,1)}), bf16[8,64,5,512]{3,0,2,1:T(8,128)(2,1)}, u32[]{:S(2)}, u32[]{:S(2)}) %all-to-all-start) | async-done | bytes 2621472 | tf_op jit(solution)/shard_map/all_to_all | solution.py:52
  223.4 4.1 %copy.65 = bf16[8,64,5,512]{3,1,2,0:T(8,128)(2,1)} copy(bf16[8,64,5,512]{3,0,2,1:T(8,128)(2,1)} %all-to-all-done) | data formatting | bytes 5242880 | tf_op jit(solution)/shard_map/all_to_all | solution.py:52
  227.5 13.8 %all-to-all-start.1 = ((bf16[8,64,5,512]{3,1,2,0:T(8,128)(2,1)}), bf16[8,64,5,512]{3,1,2,0:T(8,128)(2,1)}, u32[]{:S(2)}, u32[]{:S(2)}) async-start(bf16[8,64,5,512]{3,1,2,0:T(8,128)(2,1)} %copy.65), calls=%async_computation.1 | async-start | bytes 5242880 | tf_op jit(solution)/shard_map/all_to_all | solution.py:51
  241.3 6.7 %fusion.11 = bf16[1,768,512]{1,2,0:T(8,128)(2,1)} fusion(bf16[8,320,512]{2,0,1:T(8,128)(2,1)} %bitcast.51, bf16[8,320,768]{2,1,0:T(8,128)(2,1)} %bitcast.55), kind=kOutput, calls=%fused_computation.15 | convolution fusion | flops 2013659136 | bytes 7340032 | tf_op jit(solution)/shard_map/rnf,rnd->fd/dot_general | solution.py:59
  248.0 2.3 copy.72
  250.3 23.9 %all-to-all-done.1 = bf16[8,64,5,512]{3,1,2,0:T(8,128)(2,1)} async-done(((bf16[8,64,5,512]{3,1,2,0:T(8,128)(2,1)}), bf16[8,64,5,512]{3,1,2,0:T(8,128)(2,1)}, u32[]{:S(2)}, u32[]{:S(2)}) %all-to-all-start.1) | async-done | bytes 2621472 | tf_op jit(solution)/shard_map/all_to_all | solution.py:51
  274.2 4.8 %copy.66 = bf16[8,64,5,512]{3,0,2,1:T(8,128)(2,1)} copy(bf16[8,64,5,512]{3,1,2,0:T(8,128)(2,1)} %all-to-all-done.1) | data formatting | bytes 5242880 | tf_op jit(solution)/shard_map/all_to_all | solution.py:51
  279.0 3.8 %gather_fusion = bf16[256,8,512]{2,1,0:T(8,128)(2,1)} fusion(bf16[8,320,512]{2,0,1:T(8,128)(2,1)} %bitcast.47, s32[1024]{0:T(1024)S(1)} %pad_clamp_fusion.1), kind=kCustom, calls=%fused_computation | custom fusion | bytes 4195328 | tf_op jit(solution)/shard_map/jit(_take)/gather | solution.py:71
  282.8 6.6 %fusion.1 = (f32[128,2]{1,0:T(8,128)S(1)}, bf16[128,8,512]{2,1,0:T(8,128)(2,1)}) fusion(f32[128,8,512]{2,1,0:T(8,128)S(1)} %bitcast.44, bf16[8,128,2,512]{3,0,2,1:T(8,128)(2,1)} %bitcast.48, pred[128,2]{1,0:T(8,128)(4,1)S(1)} %copy.63, f32[128,2]{1,0:T(8,128)S(1)} %copy.59), kind=kLoop, calls=%fused_computation.6 | loop fusion | flops 5766912 | bytes 5245184 | tf_op jit(solution)/shard_map/reduce_sum | solution.py:75
  289.4 0.6 copy.73
  290.0 2.6 copy.74
  292.6 0.0 reduce-scatter.2.cloned.1.call-done
  (6 shorter events, 0.1 us)
Async XLA Ops:
  7.2 111.3 %copy-start = (bf16[1,768,512]{2,1,0:T(8,128)(2,1)S(1)}, bf16[1,768,512]{2,1,0:T(8,128)(2,1)}, u32[]{:S(2)}) copy-start(bf16[1,768,512]{2,1,0:T(8,128)(2,1)} %param.6) | copy-start | bytes 2359300
  20.3 89.6 %all-to-all-start.2 = ((bf16[8,64,5,512]{3,0,2,1:T(8,128)(2,1)}), bf16[8,64,5,512]{3,0,2,1:T(8,128)(2,1)}, u32[]{:S(2)}, u32[]{:S(2)}) async-start(bf16[8,64,5,512]{3,0,2,1:T(8,128)(2,1)} %multiply_convert_fusion), calls=%async_computation.2 | async-start | bytes 5242880 | tf_op jit(solution)/shard_map/all_to_all | solution.py:39
  35.5 82.9 %all-gather.3.cloned.1.call-start = ((), (), s32[]{:S(2)}) async-start(), calls=%async_computation.6 | async-start | bytes 4423680 | tf_op jit(solution)/shard_map/all_gather | solution.py:46
  114.0 37.2 %all-to-all-start.3 = ((bf16[8,64,5,512]{3,1,2,0:T(8,128)(2,1)}), bf16[8,64,5,512]{3,1,2,0:T(8,128)(2,1)}, u32[]{:S(2)}, u32[]{:S(2)}) async-start(bf16[8,64,5,512]{3,1,2,0:T(8,128)(2,1)} %copy.68), calls=%async_computation.3 | async-start | bytes 5242880 | tf_op jit(solution)/shard_map/all_to_all | solution.py:38
  151.2 72.2 %all-to-all-start = ((bf16[8,64,5,512]{3,0,2,1:T(8,128)(2,1)}), bf16[8,64,5,512]{3,0,2,1:T(8,128)(2,1)}, u32[]{:S(2)}, u32[]{:S(2)}) async-start(bf16[8,64,5,512]{3,0,2,1:T(8,128)(2,1)} %bitcast.46), calls=%async_computation | async-start | bytes 5242880 | tf_op jit(solution)/shard_map/all_to_all | solution.py:52
  159.1 133.5 %reduce-scatter.2.cloned.1.call-start = ((), (), s32[]{:S(2)}) async-start(), calls=%async_computation.5 | async-start | bytes 4423680 | tf_op jit(solution)/shard_map/reduce_scatter | solution.py:62
  162.5 1.6 copy-start.1
  169.2 0.7 copy-start.2
  227.5 46.7 %all-to-all-start.1 = ((bf16[8,64,5,512]{3,1,2,0:T(8,128)(2,1)}), bf16[8,64,5,512]{3,1,2,0:T(8,128)(2,1)}, u32[]{:S(2)}, u32[]{:S(2)}) async-start(bf16[8,64,5,512]{3,1,2,0:T(8,128)(2,1)} %copy.65), calls=%async_computation.1 | async-start | bytes 5242880 | tf_op jit(solution)/shard_map/all_to_all | solution.py:51
Sparse Core Ops, SparseCore 0:
  38.5 37.3 all-gather.2
  169.4 42.8 reduce-scatter.1
where the time goes:
time: 300 us; the launch traced here: 299 us
  waiting for transfers between devices  177 us (59%)
  starting transfers between devices  41.6 us (14%)
  local copies, waits for them, and re-layouts  36.7 us (12%)
  matrix products  16.2 us (5%)
  between operations  14.2 us (5%)
  other arithmetic  14.1 us (5%)
    all_to_all x1, waiting for transfers between devices, per_device(): lax.all_to_all(outgoing, 'exp', split_axis=1, concat_axis=1, tiled=True)  73.5 us
    all_to_all x1, waiting for transfers between devices, per_device(): lax.all_to_all(outputs, 'exp', split_axis=1, concat_axis=1, tiled=True)  53.1 us
    all_to_all x1, waiting for transfers between devices, per_device(): lax.all_to_all(lax.all_to_all(outgoing, 'exp', split_axis=1, concat_axis=...  25.5 us
    all_to_all x1, waiting for transfers between devices, per_device(): lax.all_to_all(lax.all_to_all(outputs, 'exp', split_axis=1, concat_axis=1...  23.9 us
    all_to_all x1, starting transfers between devices, per_device(): lax.all_to_all(outgoing, 'exp', split_axis=1, concat_axis=1, tiled=True)  15.3 us
    all_to_all x1, starting transfers between devices, per_device(): lax.all_to_all(lax.all_to_all(outputs, 'exp', split_axis=1, concat_axis=1...  13.8 us
    unnamed x11, local copies, waits for them, and re-layouts  9.37 us
    all_to_all x1, starting transfers between devices, per_device(): lax.all_to_all(outputs, 'exp', split_axis=1, concat_axis=1, tiled=True)  7.87 us
  transfers between devices with their start and end apart: 6, of which 4 were waited for; matrix products, arithmetic and copies ran while one was open for 17% of the time, Pallas kernels for 0%

commit v1 on v0

v1 whole, which is shorter than its diff:
```python
import functools

import jax
import jax.numpy as jnp
from jax import lax
from jax.experimental import pallas as pl
from jax.experimental.pallas import tpu as pltpu
from jax.sharding import PartitionSpec as P

MESH = pl.DeviceIdType.MESH
BF16 = jnp.bfloat16
F32 = jnp.float32
TOK, D, FF, CAP, SIDE, NX = 128, 4096, 768, 5, 8, 4
SRC = SIDE * SIDE
SLOTS = SRC * CAP
REP = 8
BW = D // REP
LANES = 128
GROUPS = 16
CHUNKS = ((0, 2), (2, 5))


def dot(a, b, ca, cb):
    return lax.dot_general(a, b, (((ca,), (cb,)), ((), ())), preferred_element_type=F32)


def kernel(
    hid, w, grad, ids, gates, comb_o, hg_o, dw_o, gg_o,
    S, M, R, F, wf, sgb, hp, hpT, PT, PP, dws, sibr, xs, xr, acc, hacc,
    send, recv, loc, wsend, wrecv, wloc, dsend, drecv,
):
    r = lax.axis_index("rep")
    e = lax.axis_index("exp")
    z, y = e // SIDE, e % SIDE
    x, core = r // 2, r % 2
    sib = x * 2 + 1 - core

    def zdev(t):
        return (r, t * SIDE + y)

    def ydev(t):
        return (r, z * SIDE + t)

    def xdev(t):
        return (t * 2 + core, e)

    barrier = pltpu.get_barrier_semaphore()

    def greet(o, carry):
        pl.semaphore_signal(barrier, inc=1, device_id=zdev((z + o) % SIDE), device_id_type=MESH)
        pl.semaphore_signal(barrier, inc=1, device_id=ydev((y + o) % SIDE), device_id_type=MESH)
        return carry

    lax.fori_loop(1, SIDE, greet, 0)
    for o in range(1, NX):
        pl.semaphore_signal(barrier, inc=1, device_id=xdev((x + o) % NX), device_id_type=MESH)
    pl.semaphore_signal(barrier, inc=1, device_id=(sib, e), device_id_type=MESH)

    wcopy = pltpu.make_async_copy(w, wf.at[r], wloc)
    wcopy.start()

    def alternate(i, o):
        k = (o + 1) // 2
        return (i + SIDE + k * (2 * (o % 2) - 1)) % SIDE

    def pair(a, phase, h, c0, n, t):
        cs = pl.ds(c0, n)
        if phase == 0 and h == 0:
            return S.at[a, 0, cs, t], M.at[a, 0, cs, z]
        if phase == 0:
            return S.at[a, 1, cs, :, t], M.at[a, 1, cs, y]
        if h == 0:
            return M.at[a, 0, cs, :, t], R.at[a, 0, cs, :, y]
        return M.at[a, 1, cs, :, t], R.at[a, 1, cs, z]

    def start_phase(a, phase, h, ch):
        c0, c1 = CHUNKS[ch]
        n = c1 - c0
        along_z = (phase == 0) == (h == 0)
        me = z if along_z else y

        def one(o, carry):
            t = alternate(me, o)
            s, d = pair(a, phase, h, c0, n, t)
            pltpu.make_async_remote_copy(
                src_ref=s, dst_ref=d,
                send_sem=send.at[a, phase, h], recv_sem=recv.at[a, phase, h, ch],
                device_id=zdev(t) if along_z else ydev(t), device_id_type=MESH,
            ).start()
            return carry

        lax.fori_loop(1, SIDE, one, 0)
        s, d = pair(a, phase, h, c0, n, me)
        pltpu.make_async_copy(s, d, loc.at[a, phase, h, ch]).start()

    def wait_phase(a, phase, h, ch):
        c0, c1 = CHUNKS[ch]
        n = c1 - c0
        me = z if (phase == 0) == (h == 0) else y
        s, d = pair(a, phase, h, c0, n, me)
        pltpu.make_async_copy(s, d, loc.at[a, phase, h, ch]).wait()
        land = (M if phase == 0 else R).at[a, h, pl.ds(c0, n), pl.ds(0, SIDE - 1)]
        pltpu.make_async_copy(land, land, recv.at[a, phase, h, ch]).wait()

    def wait_sent(a, phase, h):
        part = (S if phase == 0 else M).at[a, h, :, pl.ds(0, SIDE - 1)]
        pltpu.make_async_copy(part, part, send.at[a, phase, h]).wait()

    def spread(a, h):
        def one(c, carry):
            rows = F[pl.ds(pl.multiple_of(c * SRC * GROUPS, SRC * GROUPS), SRC * GROUPS), :]
            S[a, h, c] = rows.astype(BF16).reshape(SIDE, SIDE, GROUPS, LANES)
            return carry
        lax.fori_loop(0, CAP, one, 0)

    def stash(b, value):
        for j in range(BW // LANES):
            g = (b % 4) * (BW // LANES) + j
            F[pl.ds(g, SLOTS, stride=GROUPS), :] = value[:, j * LANES:(j + 1) * LANES]

    def collect(a, h, c):
        F[pl.ds(0, SRC * GROUPS), :] = R[a, h, c].reshape(SRC * GROUPS, LANES).astype(F32)
        rows = pl.ds(pl.multiple_of(c * SRC, SRC), SRC)
        for g in range(GROUPS):
            part = F[pl.ds(g, SRC, stride=GROUPS), :].astype(BF16)
            j = g % (BW // LANES)
            sgb[h * 4 + g // (BW // LANES), rows, pl.ds(j * LANES, LANES)] = part

    lane = lax.broadcasted_iota(jnp.int32, (TOK, SRC), 1)
    m0 = (ids[:, 0:1] == lane).astype(F32)
    m1 = (ids[:, 1:2] == lane).astype(F32)
    earlier = (
        lax.broadcasted_iota(jnp.int32, (TOK, TOK), 1) < lax.broadcasted_iota(jnp.int32, (TOK, TOK), 0)
    ).astype(F32).astype(BF16)
    before = dot(earlier, (m0 + m1).astype(BF16), 1, 0)
    slot_lane = lax.broadcasted_iota(jnp.int32, (TOK, SLOTS), 1)
    for k, m in ((0, m0), (1, m1)):
        position = jnp.sum(m * before, axis=1, keepdims=True).astype(jnp.int32)
        target = position * SRC + ids[:, k:k + 1]
        PP[k * TOK:(k + 1) * TOK, :] = (slot_lane == target).astype(F32).astype(BF16)
    eye = (
        lax.broadcasted_iota(jnp.int32, (2 * TOK, 2 * TOK), 0)
        == lax.broadcasted_iota(jnp.int32, (2 * TOK, 2 * TOK), 1)
    ).astype(F32).astype(BF16)
    PT[...] = dot(PP[...], eye, 0, 0).astype(BF16)
    g0, g1 = gates[:, 0:1], gates[:, 1:2]

    def gather(b, carry):
        cols = pl.ds(pl.multiple_of(b * BW, BW), BW)
        part = grad[:, cols].astype(F32)
        scaled = jnp.concatenate([(g0 * part).astype(BF16), (g1 * part).astype(BF16)], axis=0)
        stash(b, dot(PT[...], scaled, 1, 0))
        return carry

    for h in range(2):
        lax.fori_loop(4 * h, 4 * h + 4, gather, 0)
        spread(0, h)
        if h == 0:
            pl.semaphore_wait(barrier, 2 * (SIDE - 1) + NX)
        for ch in range(len(CHUNKS)):
            start_phase(0, 0, h, ch)
    wcopy.wait()

    def wmove(b, dev, i):
        return pltpu.make_async_remote_copy(
            src_ref=wf.at[b], dst_ref=wf.at[b], send_sem=wsend.at[i], recv_sem=wrecv.at[i],
            device_id=dev, device_id_type=MESH,
        )

    wx = [wmove(r, xdev((x + o) % NX), o) for o in (1, 3, 2)]
    for c in wx:
        c.start()
    wsib = [wmove(r, (sib, e), 4)]
    wsib[0].start()

    row = lax.broadcasted_iota(jnp.int32, (SLOTS, SLOTS), 0)
    col = lax.broadcasted_iota(jnp.int32, (SLOTS, SLOTS), 1)
    perm = (col == (row % SRC) * CAP + row // SRC).astype(F32).astype(BF16)
    hp[...] = dot(perm, hid[...], 1, 0).astype(BF16)
    hpT[...] = dot(hid[...], perm, 0, 1).astype(BF16)

    for ch in range(len(CHUNKS)):
        for h in range(2):
            wait_phase(0, 0, h, ch)
            start_phase(0, 1, h, ch)

    for c, o in zip(wx, (1, 3, 2)):
        c.wait()
        fwd = wmove(((x + NX - o) % NX) * 2 + core, (sib, e), 4 + o)
        fwd.start()
        wsib.append(fwd)
    for c in wsib:
        c.wait()

    def expert(b, carry):
        stash(b, dot(hp[...], wf[b], 1, 0))
        return carry

    for h in range(2):
        lax.fori_loop(4 * h, 4 * h + 4, expert, 0)
        spread(1, h)
        for ch in range(len(CHUNKS)):
            start_phase(1, 0, h, ch)

    for ch, (c0, c1) in enumerate(CHUNKS):
        for h in range(2):
            wait_phase(0, 1, h, ch)

            def take(c, carry, h=h):
                collect(0, h, c)
                return carry

            lax.fori_loop(c0, c1, take, 0)

    def dmove(src, dst, dev, i):
        return pltpu.make_async_remote_copy(
            src_ref=src, dst_ref=dst, send_sem=dsend.at[i], recv_sem=drecv.at[i],
            device_id=dev, device_id_type=MESH,
        )

    def block_grad(b):
        return dot(hpT[...], sgb[b], 1, 0)

    def for_sibling(i, carry):
        dws[i] = block_grad(i * 2 + 1 - core).astype(BF16)
        dmove(dws.at[i], sibr.at[i], (sib, e), i).start()
        return carry

    lax.fori_loop(0, NX, for_sibling, 0)

    def back(b, carry):
        hacc[...] += dot(sgb[b], wf[b], 1, 1)
        return carry

    hacc[...] = jnp.zeros_like(hacc)
    lax.fori_loop(0, REP, back, 0)
    hg_o[...] = dot(perm, hacc[...].astype(BF16), 0, 0).astype(BF16)

    def own_type(o, carry):
        t = (x + o) % NX
        dmove(dws.at[t], sibr.at[t], (sib, e), t).wait()
        xs[o] = (block_grad(t * 2 + core) + sibr[t].astype(F32)).astype(BF16)
        dmove(xs.at[o], xr.at[o], xdev(t), NX + o).start()
        return carry

    lax.fori_loop(1, NX, own_type, 0)
    dmove(dws.at[x], sibr.at[x], (sib, e), x).wait()
    acc[...] = block_grad(r) + sibr[x].astype(F32)

    for ch in range(len(CHUNKS)):
        for h in range(2):
            wait_phase(1, 0, h, ch)
            start_phase(1, 1, h, ch)

    for o in (1, 3, 2):
        dmove(xs.at[o], xr.at[o], xdev((x + o) % NX), NX + o).wait()
    dw_o[...] = (acc[...] + xr[1].astype(F32) + xr[2].astype(F32) + xr[3].astype(F32)).astype(BF16)

    for ch, (c0, c1) in enumerate(CHUNKS):
        for h in range(2):
            wait_phase(1, 1, h, ch)

            def take(c, carry, h=h):
                collect(1, h, c)
                return carry

            lax.fori_loop(c0, c1, take, 0)

    def combine(b, carry):
        s0, s1 = carry
        cols = pl.ds(pl.multiple_of(b * BW, BW), BW)
        part = grad[:, cols].astype(F32)
        p0 = dot(PP[0:TOK, :], sgb[b], 1, 0)
        p1 = dot(PP[TOK:2 * TOK, :], sgb[b], 1, 0)
        comb_o[:, cols] = (g0 * p0 + g1 * p1).astype(BF16)
        return s0 + part * p0, s1 + part * p1

    zero = jnp.zeros((TOK, BW), F32)
    s0, s1 = lax.fori_loop(0, REP, combine, (zero, zero))
    gg_o[:, 0:1] = jnp.sum(s0, axis=1, keepdims=True)
    gg_o[:, 1:2] = jnp.sum(s1, axis=1, keepdims=True)

    for a in range(2):
        for phase in range(2):
            for h in range(2):
                wait_sent(a, phase, h)


def per_device(hidden, down_weight, grad_out, expert_ids, gate_weights):
    vmem = pl.BlockSpec(memory_space=pltpu.VMEM)
    dma = pltpu.SemaphoreType.DMA
    n = len(CHUNKS)
    a2a = pltpu.VMEM((2, 2, CAP, SIDE, SIDE, GROUPS, LANES), BF16)
    quarter = pltpu.VMEM((NX, FF, BW), BF16)
    combined, hidden_grad, weight_grad, gate_grad = pl.pallas_call(
        kernel,
        out_shape=(
            jax.ShapeDtypeStruct((TOK, D), BF16),
            jax.ShapeDtypeStruct((SLOTS, FF), BF16),
            jax.ShapeDtypeStruct((FF, BW), BF16),
            jax.ShapeDtypeStruct((TOK, 2), F32),
        ),
        in_specs=[vmem] * 5,
        out_specs=(vmem,) * 4,
        scratch_shapes=[
            a2a, a2a, a2a,
            pltpu.VMEM((SLOTS * GROUPS, LANES), F32),
            pltpu.VMEM((REP, FF, BW), BF16),
            pltpu.VMEM((REP, SLOTS, BW), BF16),
            pltpu.VMEM((SLOTS, FF), BF16),
            pltpu.VMEM((FF, SLOTS), BF16),
            pltpu.VMEM((SLOTS, 2 * TOK), BF16),
            pltpu.VMEM((2 * TOK, SLOTS), BF16),
            quarter, quarter, quarter, quarter,
            pltpu.VMEM((FF, BW), F32),
            pltpu.VMEM((SLOTS, FF), F32),
            dma((2, 2, 2)), dma((2, 2, 2, n)), dma((2, 2, 2, n)),
            dma((8,)), dma((8,)), dma,
            dma((8,)), dma((8,)),
        ],
        compiler_params=pltpu.CompilerParams(
            collective_id=0, has_side_effects=True, vmem_limit_bytes=60 * 1024 * 1024
        ),
        cost_estimate=pl.CostEstimate(
            flops=7_000_000_000, bytes_accessed=5_000_000, transcendentals=0
        ),
    )(hidden[0, 0], down_weight[0], grad_out, expert_ids, gate_weights)
    return combined, hidden_grad[None, None], weight_grad[None], gate_grad


def solution(mesh):
    return jax.shard_map(
        per_device,
        mesh=mesh,
        in_specs=(
            P("rep", "exp", None, None),
            P("exp", None, "rep"),
            P(("rep", "exp"), None),
            P(("rep", "exp"), None),
            P(("rep", "exp"), None),
        ),
        out_specs=(
            P(("rep", "exp"), None),
            P("rep", "exp", None, None),
            P("exp", None, "rep"),
            P(("rep", "exp"), None),
        ),
        check_vma=False,
    )
```

time: 300 us -> 148 us (0.49)
  the two profiles are of different devices: /device:TPU:112 before, /device:TPU:6 now
where the time goes in v1:
time: 148 us; the launch traced here: 147 us
  Pallas kernels  138 us (93%)
  local copies, waits for them, and re-layouts  8.17 us (6%)
    pallas_call x1, Pallas kernels, per_device(): pl.pallas_call(kernel, out_shape=(jax.ShapeDtypeStruct((TOK, D), BF16), j...  138 us
    unnamed x14, local copies, waits for them, and re-layouts  8.17 us

profile of v1, /device:TPU:6, one launch (start us, length us, event | category | flops | bytes accessed | tf_op | source)
XLA Modules:
  0.0 147.2 jit_solution(11553340381990218952)
XLA Ops:
  0.6 0.0 copy-start.2
  0.6 0.7 copy-done.2
  1.3 0.0 copy-start.3
  1.3 0.7 copy.9.ids
  2.1 0.0 copy-done.3
  2.1 0.7 copy.10.gates
  2.8 138.4 %shard_map.84 = (bf16[128,4096]{1,0:T(8,128)(2,1)}, bf16[320,768]{1,0:T(8,128)(2,1)}, bf16[768,512]{1,0:T(8,128)(2,1)}, f32[128,2]{1,0:T(8,128)}) custom-call(bf16[320,768]{1,0:T(8,128)(2,1)} %bitcast.7, bf16[768,512]{1,0:T(8,128)(2,1)} %bitcast.6, bf16[128,4096]{1,0:T(8,128)(2,1)} %grad.1, s32[128,2]{1,0:T(8,128)} %copy.9.ids, f32[128,2]{1,0:T(8,128)} %copy.10.gates), custom_call_target="tpu_custom_call" | custom-call | flops 7000000000 | bytes 5000000 | tf_op jit(solution)/shard_map/pallas_call | solution.py:295
  141.2 1.5 %copy.11 = f32[128,2]{0,1:T(2,128)} copy(f32[128,2]{1,0:T(8,128)} %get-tuple-element.15) | data formatting | bytes 2048
  142.7 0.0 copy-start.1
  142.7 2.3 %copy.15 = bf16[128,4096]{1,0:T(8,128)(2,1)} copy(bf16[128,4096]{1,0:T(8,128)(2,1)} %get-tuple-element.20) | data formatting | bytes 2097152
  145.0 0.0 copy-done.1
  145.0 0.0 copy-start
  145.0 0.8 copy.16
  145.8 0.5 copy-done
  146.3 0.9 copy.17
Async XLA Ops:
  0.6 0.7 copy-start.2
  1.3 0.7 copy-start.3
  142.7 2.3 %copy-start.1 = (bf16[320,768]{1,0:T(8,128)(2,1)S(1)}, bf16[320,768]{1,0:T(8,128)(2,1)}, u32[]{:S(2)}) copy-start(bf16[320,768]{1,0:T(8,128)(2,1)} %get-tuple-element.9) | copy-start | bytes 1474564
  145.0 1.3 copy-start

commit v2 on v1

--- a/solution.py
+++ b/solution.py
@@ -17,7 +17,8 @@
 BW = D // REP
 LANES = 128
 GROUPS = 16
-CHUNKS = ((0, 2), (2, 5))
+CHUNKS = ((0, 2), (2, 4), (4, 5))
+ORDER = ((0, 0), (1, 0), (0, 1), (1, 1), (0, 2), (1, 2))
 
 
 def dot(a, b, ca, cb):
@@ -25,9 +26,9 @@
 
 
 def kernel(
-    hid, w, grad, ids, gates, comb_o, hg_o, dw_o, gg_o,
-    S, M, R, F, wf, sgb, hp, hpT, PT, PP, dws, sibr, xs, xr, acc, hacc,
-    send, recv, loc, wsend, wrecv, wloc, dsend, drecv,
+    hid, w, grad_in, ids, gates, comb_o, hg_o, dw_o, gg_o,
+    S, M, R, F, wf, sgb, grad, hv, hp, hpT, PT, PP, dws, sibr, xs, xr, acc, hacc, gcol, gsum, pacc,
+    send, recv, loc, wsend, wrecv, wloc, hloc, gloc, dsend, drecv,
 ):
     r = lax.axis_index("rep")
     e = lax.axis_index("exp")
@@ -56,8 +57,12 @@
         pl.semaphore_signal(barrier, inc=1, device_id=xdev((x + o) % NX), device_id_type=MESH)
     pl.semaphore_signal(barrier, inc=1, device_id=(sib, e), device_id_type=MESH)
 
+    gcopy = pltpu.make_async_copy(grad_in, grad, gloc)
+    gcopy.start()
     wcopy = pltpu.make_async_copy(w, wf.at[r], wloc)
     wcopy.start()
+    hcopy = pltpu.make_async_copy(hid, hv, hloc)
+    hcopy.start()
 
     def alternate(i, o):
         k = (o + 1) // 2
@@ -126,32 +131,31 @@
             j = g % (BW // LANES)
             sgb[h * 4 + g // (BW // LANES), rows, pl.ds(j * LANES, LANES)] = part
 
-    lane = lax.broadcasted_iota(jnp.int32, (TOK, SRC), 1)
-    m0 = (ids[:, 0:1] == lane).astype(F32)
-    m1 = (ids[:, 1:2] == lane).astype(F32)
+    expert_row = lax.broadcasted_iota(jnp.int32, (SRC, TOK), 0)
+    m0 = (ids[0:1, :] == expert_row).astype(F32)
+    m1 = (ids[1:2, :] == expert_row).astype(F32)
     earlier = (
-        lax.broadcasted_iota(jnp.int32, (TOK, TOK), 1) < lax.broadcasted_iota(jnp.int32, (TOK, TOK), 0)
+        lax.broadcasted_iota(jnp.int32, (TOK, TOK), 0) < lax.broadcasted_iota(jnp.int32, (TOK, TOK), 1)
     ).astype(F32).astype(BF16)
-    before = dot(earlier, (m0 + m1).astype(BF16), 1, 0)
-    slot_lane = lax.broadcasted_iota(jnp.int32, (TOK, SLOTS), 1)
+    before = dot((m0 + m1).astype(BF16), earlier, 1, 0)
+    slot_row = lax.broadcasted_iota(jnp.int32, (SLOTS, TOK), 0)
     for k, m in ((0, m0), (1, m1)):
-        position = jnp.sum(m * before, axis=1, keepdims=True).astype(jnp.int32)
-        target = position * SRC + ids[:, k:k + 1]
-        PP[k * TOK:(k + 1) * TOK, :] = (slot_lane == target).astype(F32).astype(BF16)
-    eye = (
-        lax.broadcasted_iota(jnp.int32, (2 * TOK, 2 * TOK), 0)
-        == lax.broadcasted_iota(jnp.int32, (2 * TOK, 2 * TOK), 1)
-    ).astype(F32).astype(BF16)
-    PT[...] = dot(PP[...], eye, 0, 0).astype(BF16)
-    g0, g1 = gates[:, 0:1], gates[:, 1:2]
+        position = jnp.sum(m * before, axis=0, keepdims=True).astype(jnp.int32)
+        target = position * SRC + ids[k:k + 1, :]
+        PT[:, k * TOK:(k + 1) * TOK] = (slot_row == target).astype(F32).astype(BF16)
+        gcol[k] = jnp.broadcast_to(gates[k:k + 1, :], (TOK, TOK)).T
+
+    def gate(k):
+        return jnp.concatenate([gcol[k]] * (BW // LANES), axis=1)
 
     def gather(b, carry):
         cols = pl.ds(pl.multiple_of(b * BW, BW), BW)
         part = grad[:, cols].astype(F32)
-        scaled = jnp.concatenate([(g0 * part).astype(BF16), (g1 * part).astype(BF16)], axis=0)
+        scaled = jnp.concatenate([(gate(0) * part).astype(BF16), (gate(1) * part).astype(BF16)], axis=0)
         stash(b, dot(PT[...], scaled, 1, 0))
         return carry
 
+    gcopy.wait()
     for h in range(2):
         lax.fori_loop(4 * h, 4 * h + 4, gather, 0)
         spread(0, h)
@@ -173,16 +177,21 @@
     wsib = [wmove(r, (sib, e), 4)]
     wsib[0].start()
 
+    eye = (
+        lax.broadcasted_iota(jnp.int32, (SLOTS, SLOTS), 0)
+        == lax.broadcasted_iota(jnp.int32, (SLOTS, SLOTS), 1)
+    ).astype(F32).astype(BF16)
+    PP[...] = dot(PT[...], eye, 0, 0).astype(BF16)
+    hcopy.wait()
     row = lax.broadcasted_iota(jnp.int32, (SLOTS, SLOTS), 0)
     col = lax.broadcasted_iota(jnp.int32, (SLOTS, SLOTS), 1)
     perm = (col == (row % SRC) * CAP + row // SRC).astype(F32).astype(BF16)
-    hp[...] = dot(perm, hid[...], 1, 0).astype(BF16)
-    hpT[...] = dot(hid[...], perm, 0, 1).astype(BF16)
-
-    for ch in range(len(CHUNKS)):
-        for h in range(2):
-            wait_phase(0, 0, h, ch)
-            start_phase(0, 1, h, ch)
+    hp[...] = dot(perm, hv[...], 1, 0).astype(BF16)
+    hpT[...] = dot(hv[...], perm, 0, 1).astype(BF16)
+
+    for h, ch in ORDER:
+        wait_phase(0, 0, h, ch)
+        start_phase(0, 1, h, ch)
 
     for c, o in zip(wx, (1, 3, 2)):
         c.wait()
@@ -202,15 +211,17 @@
         for ch in range(len(CHUNKS)):
             start_phase(1, 0, h, ch)
 
-    for ch, (c0, c1) in enumerate(CHUNKS):
-        for h in range(2):
-            wait_phase(0, 1, h, ch)
-
-            def take(c, carry, h=h):
-                collect(0, h, c)
-                return carry
-
-            lax.fori_loop(c0, c1, take, 0)
+    def take_in(a, h, ch):
+        wait_phase(a, 1, h, ch)
+
+        def take(c, carry):
+            collect(a, h, c)
+            return carry
+
+        lax.fori_loop(*CHUNKS[ch], take, 0)
+
+    for h, ch in ORDER:
+        take_in(0, h, ch)
 
     def dmove(src, dst, dev, i):
         return pltpu.make_async_remote_copy(
@@ -247,38 +258,41 @@
     dmove(dws.at[x], sibr.at[x], (sib, e), x).wait()
     acc[...] = block_grad(r) + sibr[x].astype(F32)
 
-    for ch in range(len(CHUNKS)):
-        for h in range(2):
-            wait_phase(1, 0, h, ch)
-            start_phase(1, 1, h, ch)
+    for h, ch in ORDER:
+        wait_phase(1, 0, h, ch)
+        start_phase(1, 1, h, ch)
 
     for o in (1, 3, 2):
         dmove(xs.at[o], xr.at[o], xdev((x + o) % NX), NX + o).wait()
     dw_o[...] = (acc[...] + xr[1].astype(F32) + xr[2].astype(F32) + xr[3].astype(F32)).astype(BF16)
 
-    for ch, (c0, c1) in enumerate(CHUNKS):
-        for h in range(2):
-            wait_phase(1, 1, h, ch)
-
-            def take(c, carry, h=h):
-                collect(1, h, c)
+    gsum[...] = jnp.zeros_like(gsum)
+    last = len(CHUNKS) - 1
+    for h, ch in ORDER:
+        take_in(1, h, ch)
+        rows = slice(CHUNKS[ch][0] * SRC, CHUNKS[ch][1] * SRC)
+
+        def combine(b, carry, ch=ch, rows=rows):
+            picked = dot(PP[:, rows], sgb[b, rows], 1, 0)
+            if ch > 0:
+                picked += pacc[b]
+            if ch < last:
+                pacc[b] = picked
                 return carry
-
-            lax.fori_loop(c0, c1, take, 0)
-
-    def combine(b, carry):
-        s0, s1 = carry
-        cols = pl.ds(pl.multiple_of(b * BW, BW), BW)
-        part = grad[:, cols].astype(F32)
-        p0 = dot(PP[0:TOK, :], sgb[b], 1, 0)
-        p1 = dot(PP[TOK:2 * TOK, :], sgb[b], 1, 0)
-        comb_o[:, cols] = (g0 * p0 + g1 * p1).astype(BF16)
-        return s0 + part * p0, s1 + part * p1
-
-    zero = jnp.zeros((TOK, BW), F32)
-    s0, s1 = lax.fori_loop(0, REP, combine, (zero, zero))
-    gg_o[:, 0:1] = jnp.sum(s0, axis=1, keepdims=True)
-    gg_o[:, 1:2] = jnp.sum(s1, axis=1, keepdims=True)
+            cols = pl.ds(pl.multiple_of(b * BW, BW), BW)
+            part = grad[:, cols].astype(F32)
+            p0, p1 = picked[:TOK], picked[TOK:]
+            comb_o[:, cols] = (gate(0) * p0 + gate(1) * p1).astype(BF16)
+            for k, p in ((0, p0), (1, p1)):
+                q = part * p
+                gsum[k] += (q[:, 0:LANES] + q[:, LANES:2 * LANES]) + (
+                    q[:, 2 * LANES:3 * LANES] + q[:, 3 * LANES:]
+                )
+            return carry
+
+        lax.fori_loop(4 * h, 4 * h + 4, combine, 0)
+    for k in range(2):
+        gg_o[k:k + 1, :] = jnp.sum(gsum[k].T, axis=0, keepdims=True)
 
     for a in range(2):
         for phase in range(2):
@@ -288,6 +302,7 @@
 
 def per_device(hidden, down_weight, grad_out, expert_ids, gate_weights):
     vmem = pl.BlockSpec(memory_space=pltpu.VMEM)
+    hbm = pl.BlockSpec(memory_space=pl.ANY)
     dma = pltpu.SemaphoreType.DMA
     n = len(CHUNKS)
     a2a = pltpu.VMEM((2, 2, CAP, SIDE, SIDE, GROUPS, LANES), BF16)
@@ -295,18 +310,20 @@
     combined, hidden_grad, weight_grad, gate_grad = pl.pallas_call(
         kernel,
         out_shape=(
-            jax.ShapeDtypeStruct((TOK, D), BF16),
-            jax.ShapeDtypeStruct((SLOTS, FF), BF16),
-            jax.ShapeDtypeStruct((FF, BW), BF16),
-            jax.ShapeDtypeStruct((TOK, 2), F32),
-        ),
-        in_specs=[vmem] * 5,
+            pltpu.VMEM((TOK, D), BF16),
+            pltpu.VMEM((SLOTS, FF), BF16),
+            pltpu.VMEM((FF, BW), BF16),
+            pltpu.VMEM((2, TOK), F32),
+        ),
+        in_specs=[hbm, hbm, hbm, vmem, vmem],
         out_specs=(vmem,) * 4,
         scratch_shapes=[
             a2a, a2a, a2a,
             pltpu.VMEM((SLOTS * GROUPS, LANES), F32),
             pltpu.VMEM((REP, FF, BW), BF16),
             pltpu.VMEM((REP, SLOTS, BW), BF16),
+            pltpu.VMEM((TOK, D), BF16),
+            pltpu.VMEM((SLOTS, FF), BF16),
             pltpu.VMEM((SLOTS, FF), BF16),
             pltpu.VMEM((FF, SLOTS), BF16),
             pltpu.VMEM((SLOTS, 2 * TOK), BF16),
@@ -314,18 +331,21 @@
             quarter, quarter, quarter, quarter,
             pltpu.VMEM((FF, BW), F32),
             pltpu.VMEM((SLOTS, FF), F32),
+            pltpu.VMEM((2, TOK, LANES), F32),
+            pltpu.VMEM((2, TOK, LANES), F32),
+            pltpu.VMEM((REP, 2 * TOK, BW), F32),
             dma((2, 2, 2)), dma((2, 2, 2, n)), dma((2, 2, 2, n)),
-            dma((8,)), dma((8,)), dma,
+            dma((8,)), dma((8,)), dma, dma, dma,
             dma((8,)), dma((8,)),
         ],
         compiler_params=pltpu.CompilerParams(
-            collective_id=0, has_side_effects=True, vmem_limit_bytes=60 * 1024 * 1024
+            collective_id=0, has_side_effects=True, vmem_limit_bytes=57 * 1024 * 1024
         ),
         cost_estimate=pl.CostEstimate(
             flops=7_000_000_000, bytes_accessed=5_000_000, transcendentals=0
         ),
-    )(hidden[0, 0], down_weight[0], grad_out, expert_ids, gate_weights)
-    return combined, hidden_grad[None, None], weight_grad[None], gate_grad
+    )(hidden[0, 0], down_weight[0], grad_out, expert_ids.T, gate_weights.T)
+    return combined, hidden_grad[None, None], weight_grad[None], gate_grad.T
 
 
 def solution(mesh):

time: 148 us -> 138 us (0.932)
  local copies, waits for them, and re-layouts: 8.17 us -> 3.19 us
  Pallas kernels: 138 us -> 134 us
    unnamed x14 -> x4, local copies, waits for them, and re-layouts: 8.17 us -> 3.19 us
    pallas_call x1, Pallas kernels: 138 us -> 134 us  [per_device(): pl.pallas_call(kernel, out_shape=(pltpu.VMEM((TOK, D), BF16), pltpu.VMEM(...]
where the time goes in v2:
time: 138 us
  Pallas kernels  134 us (97%)
  local copies, waits for them, and re-layouts  3.19 us (2%)
    pallas_call x1, Pallas kernels, per_device(): pl.pallas_call(kernel, out_shape=(pltpu.VMEM((TOK, D), BF16), pltpu.VMEM(...  134 us
    unnamed x4, local copies, waits for them, and re-layouts  3.19 us

profile of v2, /device:TPU:6, one launch (start us, length us, event | category | flops | bytes accessed | tf_op | source)
XLA Modules:
  0.0 138.1 jit_solution(12628499529327674484)
XLA Ops:
  0.6 134.3 %shard_map.84 = (bf16[128,4096]{1,0:T(8,128)(2,1)S(1)}, bf16[320,768]{1,0:T(8,128)(2,1)S(1)}, bf16[768,512]{1,0:T(8,128)(2,1)S(1)}, f32[2,128]{1,0:T(2,128)S(1)}) custom-call(bf16[320,768]{1,0:T(8,128)(2,1)} %bitcast.11, bf16[768,512]{1,0:T(8,128)(2,1)} %bitcast.10, bf16[128,4096]{1,0:T(8,128)(2,1)} %grad_in.1, s32[2,128]{1,0:T(2,128)} %bitcast.12, ...), custom_call_target="tpu_custom_call" | custom-call | flops 7000000000 | bytes 5000000 | tf_op jit(solution)/shard_map/pallas_call | solution.py:310
  134.9 1.0 copy.13
  135.9 0.8 copy.14
  136.7 0.6 copy.16
  137.2 0.9 copy.15

commit v3 on v2

--- a/solution.py
+++ b/solution.py
@@ -300,6 +300,15 @@
                 wait_sent(a, phase, h)
 
 
+def deliver(*refs):
+    sems = refs[-1]
+    copies = [pltpu.make_async_copy(refs[i], refs[4 + i], sems.at[i]) for i in range(4)]
+    for c in copies:
+        c.start()
+    for c in copies:
+        c.wait()
+
+
 def per_device(hidden, down_weight, grad_out, expert_ids, gate_weights):
     vmem = pl.BlockSpec(memory_space=pltpu.VMEM)
     hbm = pl.BlockSpec(memory_space=pl.ANY)
@@ -307,7 +316,7 @@
     n = len(CHUNKS)
     a2a = pltpu.VMEM((2, 2, CAP, SIDE, SIDE, GROUPS, LANES), BF16)
     quarter = pltpu.VMEM((NX, FF, BW), BF16)
-    combined, hidden_grad, weight_grad, gate_grad = pl.pallas_call(
+    held = pl.pallas_call(
         kernel,
         out_shape=(
             pltpu.VMEM((TOK, D), BF16),
@@ -345,6 +354,18 @@
             flops=7_000_000_000, bytes_accessed=5_000_000, transcendentals=0
         ),
     )(hidden[0, 0], down_weight[0], grad_out, expert_ids.T, gate_weights.T)
+    combined, hidden_grad, weight_grad, gate_grad = pl.pallas_call(
+        deliver,
+        out_shape=(
+            jax.ShapeDtypeStruct((TOK, D), BF16),
+            jax.ShapeDtypeStruct((SLOTS, FF), BF16),
+            jax.ShapeDtypeStruct((FF, BW), BF16),
+            jax.ShapeDtypeStruct((2, TOK), F32),
+        ),
+        in_specs=[vmem] * 4,
+        out_specs=(hbm,) * 4,
+        scratch_shapes=[dma((4,))],
+    )(*(pltpu.with_memory_space_constraint(a, pltpu.VMEM) for a in held))
     return combined, hidden_grad[None, None], weight_grad[None], gate_grad.T
 
 

time: 138 us -> 137 us (level)
  local copies, waits for them, and re-layouts: 3.19 us -> 0 us
  Pallas kernels: 134 us -> 136 us
    unnamed x4 -> x0, local copies, waits for them, and re-layouts: 3.19 us -> none
    pallas_call x0 -> x1, Pallas kernels: none -> 1.43 us  [per_device(): pl.pallas_call(deliver, out_shape=(jax.ShapeDtypeStruct((TOK, D), BF16),...]
where the time goes in v3:
time: 137 us; the launch traced here: 136 us
  Pallas kernels  136 us (99%)
    pallas_call x1, Pallas kernels, per_device(): pl.pallas_call(kernel, out_shape=(pltpu.VMEM((TOK, D), BF16), pltpu.VMEM(...  134 us

profile of v3, /device:TPU:6, one launch (start us, length us, event | category | flops | bytes accessed | tf_op | source)
XLA Modules:
  0.0 136.4 jit_solution(4767192538922083597)
XLA Ops:
  0.6 134.3 %shard_map.84 = (bf16[128,4096]{1,0:T(8,128)(2,1)S(1)}, bf16[320,768]{1,0:T(8,128)(2,1)S(1)}, bf16[768,512]{1,0:T(8,128)(2,1)S(1)}, f32[2,128]{1,0:T(2,128)S(1)}) custom-call(bf16[320,768]{1,0:T(8,128)(2,1)} %bitcast.9, bf16[768,512]{1,0:T(8,128)(2,1)} %bitcast.7, bf16[128,4096]{1,0:T(8,128)(2,1)} %grad_in.1, s32[2,128]{1,0:T(2,128)} %bitcast.11, ...), custom_call_target="tpu_custom_call" | custom-call | flops 7000000000 | bytes 5000000 | tf_op jit(solution)/shard_map/pallas_call | solution.py:319
  134.9 1.4 %shard_map.85 = (bf16[128,4096]{1,0:T(8,128)(2,1)}, bf16[320,768]{1,0:T(8,128)(2,1)}, bf16[768,512]{1,0:T(8,128)(2,1)}, f32[2,128]{1,0:T(2,128)}) custom-call(bf16[128,4096]{1,0:T(8,128)(2,1)S(1)} %get-tuple-element.12.refs_0_, bf16[320,768]{1,0:T(8,128)(2,1)S(1)} %get-tuple-element.13.refs_1_, bf16[768,512]{1,0:T(8,128)(2,1)S(1)} %get-tuple-element.14.refs_2_, ...), custom_call_target="tpu_custom_call" | custom-call | tf_op jit(solution)/shard_map/pallas_call | solution.py:357
